TPU v7x, 128 devices: a whole 4x4x4 slice. The times are simulated.
128 devices in a mesh: pb: 8 (over y, x_hi), kv: 16 (over z, x_lo, core).
Axes of the slice: x: 4 (x_hi: 2, x_lo: 2; x = x_hi * 2 + x_lo), y: 4, z: 4, core: 2. Of those that a mesh axis runs over, the one named last changes fastest.
Arguments:
- query_proj: bfloat16 [8192, 1024], P(('pb', 'kv')), may hold values from -6 to 6
- key_proj: bfloat16 [8192, 1024], P(('kv', 'pb')), may hold values from -8 to 8
- value_proj: bfloat16 [8192, 1024], P(('kv', 'pb')), may hold values from -6 to 6
- grad_attn: bfloat16 [8192, 1024], P(('pb', 'kv')), may hold values from -384 to 384
Outputs:
- query_grad: float32 [8192, 1024], P(('pb', 'kv'))
- key_grad: float32 [8192, 1024], P(('kv', 'pb'))
- value_grad: float32 [8192, 1024], P(('kv', 'pb'))
All inputs are finite; a program needn't handle non-finite values.
Results may differ from a plain program's by a relative error of at most 0.0095.
Values may be sent and summed in bfloat16 or wider, within the bound.
No kernel may reach another device: no remote copies, remote signals or barrier semaphores. Data moves between devices by JAX's collectives and lax.ppermute only.
A program may use at most 128 MiB of HBM per device.

v0:
```python
import jax
import jax.numpy as jnp
from jax import lax
from jax.experimental import pallas as pl
from jax.experimental.pallas import tpu as pltpu
from jax.sharding import Mesh, PartitionSpec as P

HEADS = 16
HEAD_DIM = 64
WIDE = 2 * HEAD_DIM
LOG2E = 1.4426950408889634
NN = (((1,), (0,)), ((), ()))
CHIPS = ("xl", "xh", "z", "y")
RINGS = 4
BLOCK = 64
SHARE = BLOCK // RINGS
QUERY_BLOCK = 512
GROUP = 2048
LONG = 4096
STEP = 512


def dot(left, right):
    return lax.dot_general(left, right, NN, preferred_element_type=jnp.float32)


def fold(values, op):
    return op(values.reshape(values.shape[0] // 8, 8, values.shape[1]), axis=0)


def over_rows(start, rows, step, unroll, body, carry):
    def iteration(i, carry):
        for j in range(unroll // step):
            carry = body(pl.multiple_of(start + i * unroll + j * step, step), carry)
        return carry

    return lax.fori_loop(0, rows // unroll, iteration, carry)


def operands(mine_ref, block):
    each = QUERY_BLOCK // SHARE
    qg = mine_ref[block * each : (block + 1) * each, BLOCK:, :].reshape(QUERY_BLOCK, WIDE)
    lane = lax.broadcasted_iota(jnp.int32, qg.shape, 1)
    zero = jnp.zeros_like(qg)
    query = jnp.where(lane < HEAD_DIM, qg * jnp.bfloat16(HEAD_DIM**-0.5), zero)
    return query, jnp.where(lane < HEAD_DIM, zero, qg)


def tokens_at(ref, first):
    return ref[pl.ds(first // BLOCK, STEP // BLOCK), :BLOCK, :].reshape(STEP, WIDE)


def add_scores(half, query_t, peak, keep_turned):
    kv_ref, e_ref, _, kt_ref = half

    def body(first, peak):
        kv = tokens_at(kv_ref, first)
        rows = pl.ds(first, STEP)
        scores = dot(kv, query_t) * LOG2E
        e_ref[rows, :] = scores
        if keep_turned:
            kt_ref[:, rows] = kv.T[:HEAD_DIM]
        return jnp.maximum(peak, fold(scores, jnp.max))

    rows = e_ref.shape[0]
    return over_rows(0, rows, STEP, rows, body, peak)


def add_sums(half, grad_t, peak, sums):
    kv_ref, e_ref, slope_ref, _ = half

    def body(first, carry):
        total, delta = carry
        rows = pl.ds(first, STEP)
        slopes = dot(tokens_at(kv_ref, first), grad_t)
        slope_ref[rows, :] = slopes
        e = jnp.exp2(e_ref[rows, :] - peak)
        e_ref[rows, :] = e
        return total + fold(e, jnp.sum), delta + fold(e * slopes, jnp.sum)

    return over_rows(0, e_ref.shape[0], STEP, LONG, body, sums)


def add_gradients(half, query, grad, factor, delta, put, dq_t):
    _, e_ref, slope_ref, kt_ref = half
    both = jnp.concatenate([query, grad], axis=0)

    def body(first, dq_t):
        rows = pl.ds(first, 256)
        probs = e_ref[rows, :] * factor
        weights = (probs * (slope_ref[rows, :] - delta)).astype(jnp.bfloat16)
        pair = jnp.concatenate([weights, probs.astype(jnp.bfloat16)], axis=1)
        put(rows, dot(pair, both))
        return dq_t + dot(kt_ref[:, rows], weights)

    return over_rows(0, e_ref.shape[0], 256, GROUP, body, dq_t)


def dq_rows(dq_t):
    dq = (dq_t * HEAD_DIM**-0.5).T.reshape(QUERY_BLOCK // SHARE, SHARE, HEAD_DIM)
    return jnp.concatenate([dq[:, : SHARE // 2], dq[:, SHARE // 2 :]], axis=2)


NONE = float("-inf")


def half_sums(half, query_t, grad_t, keep_turned=False):
    count = query_t.shape[1]
    none = jnp.zeros((8, count), jnp.float32)
    peak = add_scores(half, query_t, jnp.full((8, count), NONE), keep_turned)
    peak = jnp.max(peak, axis=0, keepdims=True)
    sums = add_sums(half, grad_t, peak, (none, none))
    return (peak, *(jnp.sum(x, axis=0, keepdims=True) for x in sums))


def joined(one, two):
    peak = jnp.maximum(one[0], two[0])
    first, second = jnp.exp2(one[0] - peak), jnp.exp2(two[0] - peak)
    inverse = 1.0 / (one[1] * first + two[1] * second)
    delta = (one[2] * first + two[2] * second) * inverse
    return first * inverse, second * inverse, delta


def start_kernel(mine_ref, e_ref, slope_ref, kt_ref, stat_ref):
    query, grad = operands(mine_ref, 0)
    half = (mine_ref, e_ref, slope_ref, kt_ref)
    for i, row in enumerate(half_sums(half, query.T, grad.T, keep_turned=True)):
        stat_ref[i : i + 1, :] = row


def main_kernel(
    mine_ref, pair_ref, e_in, slope_in, kt_ref, first_ref,
    e_ref, slope_ref, other_ref, own_ref, dq_ref, dqt_ref, stat_ref,
    e_pair, slope_pair, kt_pair, sum_pair,
):
    del e_in, slope_in
    mine = (mine_ref, e_ref, slope_ref, kt_ref)
    pair = (pair_ref, e_pair, slope_pair, kt_pair)

    query, grad = operands(mine_ref, 0)
    own_sums = tuple(first_ref[i : i + 1, :] for i in range(3))
    pair_sums = half_sums(pair, query.T, grad.T, keep_turned=True)
    own_factor, pair_factor, delta = joined(own_sums, pair_sums)

    def put_own(rows, part):
        own_ref[rows, :] = part

    def put_pair(rows, part):
        sum_pair[rows, :] = part

    dq_t = jnp.zeros(dqt_ref.shape, jnp.float32)
    dq_t = add_gradients(mine, query, grad, own_factor, delta, put_own, dq_t)
    dq_t = add_gradients(pair, query, grad, pair_factor, delta, put_pair, dq_t)
    dq_ref[...] = dq_rows(dq_t)

    query, grad = operands(mine_ref, 1)
    query_t, grad_t = query.T, grad.T
    own_sums = half_sums(mine, query_t, grad_t)
    pair_sums = half_sums(pair, query_t, grad_t)
    own_factor, pair_factor, delta = joined(own_sums, pair_sums)

    def put_other(rows, part):
        other_ref[rows, :] = (sum_pair[rows, :] + part).astype(other_ref.dtype)

    dqt_ref[...] = add_gradients(
        pair, query, grad, pair_factor, delta, put_other, jnp.zeros(dqt_ref.shape, jnp.float32)
    )
    stat_ref[0:1, :] = own_factor
    stat_ref[1:2, :] = delta


def end_kernel(
    mine_ref, e_ref, slope_ref, kt_ref, own_in, dqt_ref, stat_ref, own_ref, dq_ref
):
    def put(rows, part):
        own_ref[rows, :] = own_in[rows, :] + part

    query, grad = operands(mine_ref, 1)
    dq_t = add_gradients(
        (mine_ref, e_ref, slope_ref, kt_ref),
        query, grad, stat_ref[0:1, :], stat_ref[1:2, :], put, dqt_ref[...],
    )
    dq_ref[...] = dq_rows(dq_t)


def call(kernel, arrays, outs, scratch=(), limit=8, aliases=None, space=pltpu.VMEM):
    return pl.pallas_call(
        kernel,
        in_specs=[pl.BlockSpec(memory_space=pltpu.VMEM)] * len(arrays),
        out_specs=[pl.BlockSpec(memory_space=pltpu.VMEM)] * len(outs),
        out_shape=[out if hasattr(out, "dtype") else pltpu.VMEM(*out) for out in outs],
        scratch_shapes=[pltpu.VMEM(*shape) for shape in scratch],
        input_output_aliases=aliases or {},
        compiler_params=pltpu.CompilerParams(vmem_limit_bytes=limit * 2**20),
    )(*(pltpu.with_memory_space_constraint(x, space) for x in arrays))


def pack_kernel(q_ref, k_ref, v_ref, g_ref, out_ref):
    for head in range(HEADS):
        columns = slice(head * HEAD_DIM, (head + 1) * HEAD_DIM)
        kv = jnp.concatenate([k_ref[:, columns], v_ref[:, columns]], axis=1)
        qg = jnp.concatenate([q_ref[:, columns], g_ref[:, columns]], axis=1)
        for ring in range(RINGS):
            out_ref[head * RINGS + ring, :BLOCK] = kv
            out_ref[head * RINGS + ring, BLOCK:] = qg[ring * SHARE : (ring + 1) * SHARE]


def pack(query, key, value, grad):
    shape = (RINGS * HEADS, BLOCK + SHARE, WIDE)
    return call(pack_kernel, (query, key, value, grad), [(shape, query.dtype)], space=pltpu.HBM)[0]


def unpack_kernel(in_ref, dq_ref, dk_ref, dv_ref):
    each = in_ref.shape[1] // 2
    for pair in range(HEADS // 2):
        columns = slice(pair * WIDE, (pair + 1) * WIDE)
        sums = [0.0, 0.0]
        for twice in range(RINGS // 2):
            found = [
                in_ref[(2 * pair + i) * RINGS // 2 + twice].astype(jnp.float32) for i in range(2)
            ]
            for j in range(2):
                one, two = (x[j * each : (j + 1) * each] for x in found)
                sums = [sums[0] + one[:BLOCK], sums[1] + two[:BLOCK]]
                one, two = one[BLOCK:], two[BLOCK:]
                first = (2 * twice + j) * SHARE
                dq_ref[first : first + SHARE // 2, columns] = jnp.concatenate(
                    [one[:, :HEAD_DIM], two[:, :HEAD_DIM]], axis=1
                )
                dq_ref[first + SHARE // 2 : first + SHARE, columns] = jnp.concatenate(
                    [one[:, HEAD_DIM:], two[:, HEAD_DIM:]], axis=1
                )
        one, two = sums
        dk_ref[:, columns] = jnp.concatenate([one[:, :HEAD_DIM], two[:, :HEAD_DIM]], axis=1)
        dv_ref[:, columns] = jnp.concatenate([one[:, HEAD_DIM:], two[:, HEAD_DIM:]], axis=1)


def unpack(parts):
    out = jax.ShapeDtypeStruct((BLOCK, HEADS * HEAD_DIM), jnp.float32)
    return call(unpack_kernel, (parts,), [out] * 3)


def combine_kernel(own_ref, other_ref, dq0_ref, dq1_ref, out_ref):
    total = own_ref[...] + other_ref[...].astype(jnp.float32)
    total = total.reshape(-1, 2, BLOCK, WIDE)
    each = dq0_ref.shape[0] // 2
    for ref, first in ((dq0_ref, 0), (dq1_ref, each)):
        here = total[first : first + each]
        dq = ref[...].reshape(each, 2, SHARE // 2, WIDE)
        rows = [here[:, 0], dq[:, 0], here[:, 1], dq[:, 1]]
        out_ref[first : first + each] = jnp.concatenate(rows, axis=1).astype(out_ref.dtype)


def per_device(query_proj, key_proj, value_proj, grad_attn):
    low, full = jnp.bfloat16, jnp.float32

    def spread(packed):
        return lax.all_to_all(packed, CHIPS, 0, 0, tiled=True)

    def swap(values):
        return lax.ppermute(values, "core", [(0, 1), (1, 0)])

    mine = spread(pack(query_proj, key_proj, value_proj, grad_attn))
    half = mine.shape[0] * BLOCK
    wide = ((half, QUERY_BLOCK), full)
    turned = ((HEAD_DIM, half), low)
    total = ((half, WIDE), full)
    dq_shape = ((QUERY_BLOCK // SHARE, SHARE // 2, WIDE), full)
    dqt = ((HEAD_DIM, QUERY_BLOCK), full)
    eight = ((8, QUERY_BLOCK), full)
    pair = swap(mine)
    e, slope, kt, first = call(start_kernel, (mine,), [wide, wide, turned, eight])
    e, slope, other, own, dq0, dq_t, stats = call(
        main_kernel,
        (mine, pair, e, slope, kt, first),
        [wide, wide, ((half, WIDE), low), total, dq_shape, dqt, eight],
        scratch=[wide, wide, turned, total],
        limit=22,
        aliases={2: 0, 3: 1},
    )
    other = swap(other)
    own, dq1 = call(
        end_kernel, (mine, e, slope, kt, own, dq_t, stats), [total, dq_shape], aliases={4: 0}
    )
    sources, each = mine.shape[0], BLOCK + SHARE // 2
    shape = (sources // 2, 2 * each, WIDE)
    back = call(combine_kernel, (own, other, dq0, dq1), [(shape, low)])[0]
    back = spread(back.reshape(sources, each, WIDE))
    return tuple(unpack(back.reshape(shape)))


def solution(mesh):
    fine = Mesh(
        mesh.devices.reshape(RINGS, 2, 4, 2, 2), ("y", "xh", "z", "xl", "core")
    )
    queries = P(("y", "xh", "z", "xl", "core"), None)
    tokens = P(("z", "xl", "core", "y", "xh"), None)
    return jax.shard_map(
        per_device,
        mesh=fine,
        in_specs=(queries, tokens, tokens, queries),
        out_specs=(queries, tokens, tokens),
        check_vma=False,
    )
```

profile of v0, /device:TPU:0, one launch (start us, length us, event | category | flops | bytes accessed | tf_op | source)
XLA Modules:
  0.0 84.3 jit_solution(14607097397963747906)
XLA Ops:
  0.6 1.3 %shard_map.67 = bf16[64,80,128]{2,1,0:T(8,128)(2,1)S(1)} custom-call(bf16[64,1024]{1,0:T(8,128)(2,1)} %q_ref.1, bf16[64,1024]{1,0:T(8,128)(2,1)} %k_ref.1, bf16[64,1024]{1,0:T(8,128)(2,1)} %v_ref.1, bf16[64,1024]{1,0:T(8,128)(2,1)} %g_ref.1), custom_call_target="tpu_custom_call" | custom-call | tf_op jit(solution)/shard_map/pallas_call | solution.py:187
  2.0 32.7 %all_to_all.10.mine_ref = bf16[64,80,128]{2,1,0:T(8,128)(2,1)S(1)} all-to-all(bf16[64,80,128]{2,1,0:T(8,128)(2,1)S(1)} %shard_map.67), channel_id=1, replica_groups=mesh['y'=4,'xh'=2,'z'=4,'xl'=2,'core'=2] {'xl','xh','z','y'}, dimensions={0} | all-to-all | bytes 2621440 | tf_op jit(solution)/shard_map/all_to_all | solution.py:258
  34.7 0.0 collective-permute-start
  34.7 2.8 %shard_map.68 = (f32[4096,512]{1,0:T(8,128)S(1)}, f32[4096,512]{1,0:T(8,128)S(1)}, bf16[64,4096]{1,0:T(8,128)(2,1)S(1)}, f32[8,512]{1,0:T(8,128)S(1)}) custom-call(bf16[64,80,128]{2,1,0:T(8,128)(2,1)S(1)} %all_to_all.10.mine_ref), custom_call_target="tpu_custom_call" | custom-call | tf_op jit(solution)/shard_map/pallas_call | solution.py:187
  37.5 0.2 collective-permute-done.pair_ref
  37.7 16.9 %shard_map.69 = (f32[4096,512]{1,0:T(8,128)S(1)}, f32[4096,512]{1,0:T(8,128)S(1)}, bf16[4096,128]{1,0:T(8,128)(2,1)S(1)}, f32[4096,128]{1,0:T(8,128)S(1)}, f32[3...) custom-call(bf16[64,80,128]{2,1,0:T(8,128)(2,1)S(1)} %all_to_all.10., ...), custom_call_target="tpu_custom_call", output_to_operand_aliasing={{0}: (2, {}), {1}: (3, {})} | custom-call | tf_op jit(solution)/shard_map/pallas_call | solution.py:187
  54.6 0.4 collective-permute-start.1
  55.0 3.2 %shard_map.70 = (f32[4096,128]{1,0:T(8,128)S(1)}, f32[32,8,128]{2,1,0:T(8,128)S(1)}) custom-call(bf16[64,80,128]{2,1,0:T(8,128)(2,1)S(1)} %all_to_all.10.mine_ref, f32[4096,512]{1,0:T(8,128)S(1)} %get-tuple-element.20.e_ref, f32[4096,512]{1,0:T(8,128)S(1)} %get-tuple-element.21.slope_ref, ...), custom_call_target="tpu_custom_call", output_to_operand_aliasing={{0}: (4, {})} | custom-call | tf_op jit(solution)/shard_map/pallas_call | solution.py:187
  58.2 0.0 collective-permute-done.1.other_ref
  58.2 0.2 shard_map.71
  58.4 24.9 %all_to_all.11 = bf16[64,72,128]{2,1,0:T(8,128)(2,1)S(1)} all-to-all(bf16[64,72,128]{2,1,0:T(8,128)(2,1)S(1)} %bitcast.2), channel_id=1, replica_groups=mesh['y'=4,'xh'=2,'z'=4,'xl'=2,'core'=2] {'xl','xh','z','y'}, dimensions={0} | all-to-all | bytes 2359296 | tf_op jit(solution)/shard_map/all_to_all | solution.py:258
  83.2 1.1 %shard_map.72 = (f32[64,1024]{1,0:T(8,128)}, f32[64,1024]{1,0:T(8,128)}, f32[64,1024]{1,0:T(8,128)}) custom-call(bf16[32,144,128]{2,1,0:T(8,128)(2,1)S(1)} %bitcast.3), custom_call_target="tpu_custom_call" | custom-call | tf_op jit(solution)/shard_map/pallas_call | solution.py:187
Async XLA Ops:
  34.7 3.0 %collective-permute-start = (bf16[64,80,128]{2,1,0:T(8,128)(2,1)S(1)}, bf16[64,80,128]{2,1,0:T(8,128)(2,1)S(1)}, u32[]{:S(2)}, u32[]{:S(2)}) collective-permute-start(bf16[64,80,128]{2,1,0:T(8,128)(2,1)S(1)} %all_to_all.10.mine_ref), channel_id=1, source_target_pairs={{0,1},{1,0},{2,3},{3,2},{4,5},{5,4},{6,7},{7,6},{8,9},{9,8},{10,11... | collective-permute-start | bytes 3932168 | tf_op jit(solution)/shard_map/ppermute | solution.py:261
  54.6 3.5 %collective-permute-start.1 = (bf16[4096,128]{1,0:T(8,128)(2,1)S(1)}, bf16[4096,128]{1,0:T(8,128)(2,1)S(1)}, u32[]{:S(2)}, u32[]{:S(2)}) collective-permute-start(bf16[4096,128]{1,0:T(8,128)(2,1)S(1)} %get-tuple-element.26), channel_id=1, source_target_pairs={{0,1},{1,0},{2,3},{3,2},{4,5},{5,4},{6,7},{7,6},{8,9},{9,8},{10,11... | collective-permute-start | bytes 3145736 | tf_op jit(solution)/shard_map/ppermute | solution.py:261
where the time goes:
time: 84.5 us; the launch traced here: 84.3 us
  blocking collectives  57.6 us (68%)
  Pallas kernels  25.4 us (30%)
    all_to_all x2, blocking collectives, spread(): return lax.all_to_all(packed, CHIPS, 0, 0, tiled=True)  57.6 us
    pallas_call x6, Pallas kernels, call(): pl.pallas_call(kernel, in_specs=[pl.BlockSpec(memory_space=pltpu.VMEM)] *...  25.4 us
  transfers between devices with their start and end apart: 2, of which 1 were waited for; matrix products, arithmetic and copies ran while one was open for 0% of the time, Pallas kernels for 7%

commit v1 on v0

--- a/solution.py
+++ b/solution.py
@@ -81,19 +81,21 @@
     return over_rows(0, e_ref.shape[0], STEP, LONG, body, sums)
 
 
-def add_gradients(half, query, grad, factor, delta, put, dq_t):
+def add_gradients(half, query, grad, factor, delta, put, dq_t, unroll=GROUP):
     _, e_ref, slope_ref, kt_ref = half
-    both = jnp.concatenate([query, grad], axis=0)
+    parts = [slice(i, i + QUERY_BLOCK // 2) for i in (0, QUERY_BLOCK // 2)]
+    both = jnp.concatenate([x[part] for part in parts for x in (query, grad)], axis=0)
 
     def body(first, dq_t):
         rows = pl.ds(first, 256)
         probs = e_ref[rows, :] * factor
         weights = (probs * (slope_ref[rows, :] - delta)).astype(jnp.bfloat16)
-        pair = jnp.concatenate([weights, probs.astype(jnp.bfloat16)], axis=1)
-        put(rows, dot(pair, both))
+        low = probs.astype(jnp.bfloat16)
+        pair = [x[:, part] for part in parts for x in (weights, low)]
+        put(rows, dot(jnp.concatenate(pair, axis=1), both))
         return dq_t + dot(kt_ref[:, rows], weights)
 
-    return over_rows(0, e_ref.shape[0], 256, GROUP, body, dq_t)
+    return over_rows(0, e_ref.shape[0], 256, unroll, body, dq_t)
 
 
 def dq_rows(dq_t):
@@ -178,7 +180,7 @@
     query, grad = operands(mine_ref, 1)
     dq_t = add_gradients(
         (mine_ref, e_ref, slope_ref, kt_ref),
-        query, grad, stat_ref[0:1, :], stat_ref[1:2, :], put, dqt_ref[...],
+        query, grad, stat_ref[0:1, :], stat_ref[1:2, :], put, dqt_ref[...], LONG,
     )
     dq_ref[...] = dq_rows(dq_t)
 

time: 84.5 us -> 84.4 us (level)
  no operation moved by 1% of the time
where the time goes in v1:
time: 84.4 us; the launch traced here: 84.2 us
  blocking collectives  57.6 us (68%)
  Pallas kernels  25.1 us (30%)
    all_to_all x2, blocking collectives, spread(): return lax.all_to_all(packed, CHIPS, 0, 0, tiled=True)  57.6 us
    pallas_call x6, Pallas kernels, call(): pl.pallas_call(kernel, in_specs=[pl.BlockSpec(memory_space=pltpu.VMEM)] *...  25.1 us
  transfers between devices with their start and end apart: 2, of which 1 were waited for; matrix products, arithmetic and copies ran while one was open for 0% of the time, Pallas kernels for 7%

profile of v1, /device:TPU:0, one launch (start us, length us, event | category | flops | bytes accessed | tf_op | source)
XLA Modules:
  0.0 84.2 jit_solution(6539023747180744961)
XLA Ops:
  0.6 1.3 %shard_map.67 = bf16[64,80,128]{2,1,0:T(8,128)(2,1)S(1)} custom-call(bf16[64,1024]{1,0:T(8,128)(2,1)} %q_ref.1, bf16[64,1024]{1,0:T(8,128)(2,1)} %k_ref.1, bf16[64,1024]{1,0:T(8,128)(2,1)} %v_ref.1, bf16[64,1024]{1,0:T(8,128)(2,1)} %g_ref.1), custom_call_target="tpu_custom_call" | custom-call | tf_op jit(solution)/shard_map/pallas_call | solution.py:189
  2.0 32.7 %all_to_all.10.mine_ref = bf16[64,80,128]{2,1,0:T(8,128)(2,1)S(1)} all-to-all(bf16[64,80,128]{2,1,0:T(8,128)(2,1)S(1)} %shard_map.67), channel_id=1, replica_groups=mesh['y'=4,'xh'=2,'z'=4,'xl'=2,'core'=2] {'xl','xh','z','y'}, dimensions={0} | all-to-all | bytes 2621440 | tf_op jit(solution)/shard_map/all_to_all | solution.py:260
  34.7 0.0 collective-permute-start
  34.7 2.8 %shard_map.68 = (f32[4096,512]{1,0:T(8,128)S(1)}, f32[4096,512]{1,0:T(8,128)S(1)}, bf16[64,4096]{1,0:T(8,128)(2,1)S(1)}, f32[8,512]{1,0:T(8,128)S(1)}) custom-call(bf16[64,80,128]{2,1,0:T(8,128)(2,1)S(1)} %all_to_all.10.mine_ref), custom_call_target="tpu_custom_call" | custom-call | tf_op jit(solution)/shard_map/pallas_call | solution.py:189
  37.5 0.2 collective-permute-done.pair_ref
  37.7 16.7 %shard_map.69 = (f32[4096,512]{1,0:T(8,128)S(1)}, f32[4096,512]{1,0:T(8,128)S(1)}, bf16[4096,128]{1,0:T(8,128)(2,1)S(1)}, f32[4096,128]{1,0:T(8,128)S(1)}, f32[3...) custom-call(bf16[64,80,128]{2,1,0:T(8,128)(2,1)S(1)} %all_to_all.10., ...), custom_call_target="tpu_custom_call", output_to_operand_aliasing={{0}: (2, {}), {1}: (3, {})} | custom-call | tf_op jit(solution)/shard_map/pallas_call | solution.py:189
  54.5 0.6 collective-permute-start.1
  55.0 3.0 %shard_map.70 = (f32[4096,128]{1,0:T(8,128)S(1)}, f32[32,8,128]{2,1,0:T(8,128)S(1)}) custom-call(bf16[64,80,128]{2,1,0:T(8,128)(2,1)S(1)} %all_to_all.10.mine_ref, f32[4096,512]{1,0:T(8,128)S(1)} %get-tuple-element.20.e_ref, f32[4096,512]{1,0:T(8,128)S(1)} %get-tuple-element.21.slope_ref, ...), custom_call_target="tpu_custom_call", output_to_operand_aliasing={{0}: (4, {})} | custom-call | tf_op jit(solution)/shard_map/pallas_call | solution.py:189
  58.1 0.0 collective-permute-done.1.other_ref
  58.1 0.2 shard_map.71
  58.3 24.8 %all_to_all.11 = bf16[64,72,128]{2,1,0:T(8,128)(2,1)S(1)} all-to-all(bf16[64,72,128]{2,1,0:T(8,128)(2,1)S(1)} %bitcast.2), channel_id=1, replica_groups=mesh['y'=4,'xh'=2,'z'=4,'xl'=2,'core'=2] {'xl','xh','z','y'}, dimensions={0} | all-to-all | bytes 2359296 | tf_op jit(solution)/shard_map/all_to_all | solution.py:260
  83.1 1.1 %shard_map.72 = (f32[64,1024]{1,0:T(8,128)}, f32[64,1024]{1,0:T(8,128)}, f32[64,1024]{1,0:T(8,128)}) custom-call(bf16[32,144,128]{2,1,0:T(8,128)(2,1)S(1)} %bitcast.3), custom_call_target="tpu_custom_call" | custom-call | tf_op jit(solution)/shard_map/pallas_call | solution.py:189
Async XLA Ops:
  34.7 3.0 %collective-permute-start = (bf16[64,80,128]{2,1,0:T(8,128)(2,1)S(1)}, bf16[64,80,128]{2,1,0:T(8,128)(2,1)S(1)}, u32[]{:S(2)}, u32[]{:S(2)}) collective-permute-start(bf16[64,80,128]{2,1,0:T(8,128)(2,1)S(1)} %all_to_all.10.mine_ref), channel_id=1, source_target_pairs={{0,1},{1,0},{2,3},{3,2},{4,5},{5,4},{6,7},{7,6},{8,9},{9,8},{10,11... | collective-permute-start | bytes 3932168 | tf_op jit(solution)/shard_map/ppermute | solution.py:263
  54.5 3.6 %collective-permute-start.1 = (bf16[4096,128]{1,0:T(8,128)(2,1)S(1)}, bf16[4096,128]{1,0:T(8,128)(2,1)S(1)}, u32[]{:S(2)}, u32[]{:S(2)}) collective-permute-start(bf16[4096,128]{1,0:T(8,128)(2,1)S(1)} %get-tuple-element.26), channel_id=1, source_target_pairs={{0,1},{1,0},{2,3},{3,2},{4,5},{5,4},{6,7},{7,6},{8,9},{9,8},{10,11... | collective-permute-start | bytes 3145736 | tf_op jit(solution)/shard_map/ppermute | solution.py:263
